TPU v7x, 768 devices: a whole 4x8x12 slice. The times are simulated.
768 devices in a mesh: frame: 48 (over y_lo, z), height: 16 (over y_hi, x, core).
Axes of the slice: x: 4, y: 8 (y_hi: 2, y_lo: 4; y = y_hi * 4 + y_lo), z: 12, core: 2. Of those that a mesh axis runs over, the one named last changes fastest.
Arguments:
- latents: bfloat16 [48, 96, 64, 1152], P('frame', 'height'), may hold values from -30 to 30
- qkv_weight: bfloat16 [2, 1152, 1728], replicated, as said below
- out_weight: bfloat16 [2, 576, 1152], replicated, may hold values from -0.25 to 0.25
Outputs:
- result: bfloat16 [48, 96, 64, 1152], P('frame', 'height')
Inputs may be any that keep to these rules, and one draw needn't show every extreme that they name: `qkv_weight`: entries lie within -0.2 to 0.2.
All inputs are finite; a program needn't handle non-finite values.
Results may differ from a plain program's by a relative error of at most 0.0095.
Values may be sent and summed in bfloat16 or wider, within the bound.
A program may use at most 64 MiB of HBM per device.

v0:
```python
import jax
import jax.numpy as jnp
from jax import lax
from jax.sharding import PartitionSpec as P

HEAD_DIM = 72


def layer_norm(values):
    values = values.astype(jnp.float32)
    center = values - jnp.mean(values, axis=-1, keepdims=True)
    spread = jnp.mean(center * center, axis=-1, keepdims=True)
    return (center * lax.rsqrt(spread + 1e-06)).astype(jnp.bfloat16)


def project(tokens, weight):
    normed = layer_norm(tokens)
    flattened = normed.reshape(-1, normed.shape[-1])
    joined = jnp.dot(flattened, weight, preferred_element_type=jnp.float32)
    return joined.astype(jnp.bfloat16).reshape(tokens.shape[:-1] + (weight.shape[1],))


def attend(joined):
    length, batches = (joined.shape[0], joined.shape[1])
    inner_width = joined.shape[2] // 3
    head_count = inner_width // HEAD_DIM
    query_rows = joined[:, :, :inner_width].reshape(length, batches, head_count, HEAD_DIM)
    key_rows = joined[:, :, inner_width : 2 * inner_width].reshape(
        length, batches, head_count, HEAD_DIM
    )
    value_rows = joined[:, :, 2 * inner_width :].reshape(length, batches, head_count, HEAD_DIM)
    scores = jnp.einsum(
        "lbnd,mbnd->bnlm", query_rows, key_rows, preferred_element_type=jnp.float32
    ) * HEAD_DIM ** (-0.5)
    scores = scores - jnp.max(scores, axis=-1, keepdims=True)
    exponent = jnp.exp(scores)
    weights = (exponent / jnp.sum(exponent, axis=-1, keepdims=True)).astype(jnp.bfloat16)
    mixture = jnp.einsum("bnlm,mbnd->lbnd", weights, value_rows, preferred_element_type=jnp.float32)
    return mixture.reshape(length, batches, inner_width).astype(jnp.bfloat16)


def residual(tokens, mixture, weight):
    update = jnp.dot(
        mixture.reshape(-1, mixture.shape[-1]), weight, preferred_element_type=jnp.float32
    )
    return (tokens.astype(jnp.float32) + update.reshape(tokens.shape)).astype(jnp.bfloat16)


def frames_block(joined):
    length, single, places, triple = joined.shape
    mixture = attend(joined.reshape(length, single * places, triple))
    return mixture.reshape(length, single, places, triple // 3)


def per_device(latents, qkv_weight, out_weight):
    frames_dev, rows_dev, columns, feature_width = latents.shape
    frame_count = lax.axis_size("frame")
    rows_attend = jax.vmap(attend)
    joined = project(latents, qkv_weight[0])
    rows_att = rows_attend(
        lax.all_to_all(joined, "height", split_axis=2, concat_axis=1, tiled=True)
    )
    rows_att = lax.all_to_all(rows_att, "height", split_axis=1, concat_axis=2, tiled=True)
    middle = residual(latents, rows_att, out_weight[0])
    places_dev = rows_dev * columns // frame_count
    grouped = middle.reshape(frames_dev, frame_count, places_dev, feature_width)
    joined = project(grouped, qkv_weight[1])
    frames_att = frames_block(
        lax.all_to_all(joined, "frame", split_axis=1, concat_axis=0, tiled=True)
    )
    frames_att = lax.all_to_all(frames_att, "frame", split_axis=0, concat_axis=1, tiled=True)
    frames_att = frames_att.reshape(frames_dev, rows_dev, columns, frames_att.shape[-1])
    return residual(middle, frames_att, out_weight[1])


def solution(mesh):
    return jax.shard_map(
        per_device,
        mesh=mesh,
        in_specs=(P("frame", "height", None, None), P(), P()),
        out_specs=P("frame", "height", None, None),
        check_vma=False,
    )
```

profile of v0, /device:TPU:16, one launch (start us, length us, event | category | flops | bytes accessed | tf_op | source)
XLA Modules:
  0.0 223.4 jit_solution(9812636514079717283)
XLA Ops:
  0.0 1.4 convert_reduce_fusion
  1.5 1.5 fusion.21
  3.0 0.3 fusion.22
  3.3 5.6 %fusion.12 = bf16[384,1728]{0,1:T(8,128)(2,1)} fusion(bf16[384,1152]{1,0:T(8,128)(2,1)S(1)} %bitcast.79, bf16[2,1152,1728]{1,2,0:T(8,128)(2,1)} %param.4), kind=kOutput, calls=%fused_computation.14 | convolution fusion | flops 1529487360 | bytes 6193152 | tf_op jit(solution)/shard_map/dot_general | solution.py:19
  8.9 1.8 copy.22
  10.7 0.8 copy.23
  11.4 44.1 %all_to_all.51 = bf16[1,6,64,1728]{3,1,0,2:T(8,128)(2,1)S(1)} all-to-all(bf16[1,6,64,1728]{3,1,0,2:T(8,128)(2,1)S(1)} %copy.23), channel_id=1, replica_groups=mesh['frame'=48,'height'=16] {'height'}, dimensions={2} | all-to-all | bytes 2654208 | tf_op jit(solution)/shard_map/all_to_all | solution.py:61
  55.6 0.5 copy.62
  56.1 0.5 copy.25
  56.6 0.7 fusion.49
  57.3 0.4 copy.27
  57.7 0.4 copy.28
  58.2 1.2 copy.26
  59.4 1.9 fusion.50
  61.3 1.9 convolution_convert_fusion.1
  63.2 0.3 copy.30
  63.5 17.0 %all_to_all.52 = bf16[1,96,4,576]{3,2,0,1:T(4,128)(2,1)S(1)} all-to-all(bf16[1,96,4,576]{3,2,0,1:T(4,128)(2,1)S(1)} %copy.30), channel_id=1, replica_groups=mesh['frame'=48,'height'=16] {'height'}, dimensions={1} | all-to-all | bytes 884736 | tf_op jit(solution)/shard_map/all_to_all | solution.py:63
  81.0 2.3 %fusion.51 = (f32[6,64]{1,0:T(8,128)S(1)}, f32[1,6,64,1152]{3,2,1,0:T(8,128)S(1)}) fusion(bf16[6,64,576]{2,1,0:T(8,128)(2,1)S(1)} %reshape.199, bf16[2,576,1152]{2,1,0:T(8,128)(2,1)} %param.5, bf16[1,6,64,1152]{3,2,1,0:T(8,128)(2,1)S(1)} %copy-done), kind=kOutput, calls=%fused_computation.56 | convolution fusion | flops 511819392 | bytes 4425216 | tf_op jit(solution)/shard_map/dot_general | solution.py:43
  83.3 0.3 multiply_reduce_fusion
  83.6 0.2 multiply_convert_fusion
  83.9 5.6 %fusion.15 = bf16[384,1728]{0,1:T(8,128)(2,1)} fusion(bf16[384,1152]{1,0:T(8,128)(2,1)S(1)} %bitcast.80, bf16[2,1152,1728]{1,2,0:T(8,128)(2,1)} %param.4), kind=kOutput, calls=%fused_computation.15 | convolution fusion | flops 1529487360 | bytes 6193152 | tf_op jit(solution)/shard_map/dot_general | solution.py:19
  89.4 1.8 copy.32
  91.2 87.1 %all_to_all.53 = bf16[1,48,8,1728]{3,2,0,1:T(8,128)(2,1)S(1)} all-to-all(bf16[1,48,8,1728]{3,2,0,1:T(8,128)(2,1)S(1)} %bitcast.75), channel_id=1, replica_groups=mesh['frame'=48,'height'=16] {'frame'}, dimensions={1} | all-to-all | bytes 2654208 | tf_op jit(solution)/shard_map/all_to_all | solution.py:69
  178.3 0.3 fusion.48
  178.6 1.7 reshape.203
  180.2 1.7 reshape.204
  181.9 1.7 reshape.202
  183.6 3.7 %fusion.52 = (f32[8,8,48]{2,1,0:T(8,128)S(1)}, f32[8,8,48,48]{2,3,1,0:T(8,128)}) fusion(bf16[48,8,8,72]{3,2,1,0:T(8,128)(2,1)} %reshape.204, bf16[48,8,8,72]{3,2,1,0:T(8,128)(2,1)S(1)} %copy-done.1), kind=kOutput, calls=%fused_computation.57 | convolution fusion | flops 21676080 | bytes 1486848 | tf_op jit(solution)/shard_map/sub | solution.py:35
  187.3 2.2 fusion.31
  189.7 0.6 convert_element_type.99
  190.3 29.9 %all_to_all.54 = bf16[48,1,8,576]{3,2,1,0:T(8,128)(2,1)S(1)} all-to-all(bf16[48,1,8,576]{3,2,1,0:T(8,128)(2,1)S(1)} %bitcast.78), channel_id=1, replica_groups=mesh['frame'=48,'height'=16] {'frame'}, dimensions={0} | all-to-all | bytes 884736 | tf_op jit(solution)/shard_map/all_to_all | solution.py:71
  220.2 3.2 %fusion.11 = bf16[1,6,64,1152]{3,2,1,0:T(8,128)(2,1)} fusion(f32[1,6,64,1152]{3,2,1,0:T(8,128)S(1)} %get-tuple-element.14, bf16[6,64,576]{2,1,0:T(8,128)(2,1)S(1)} %bitcast.76, bf16[2,576,1152]{2,1,0:T(8,128)(2,1)} %param.5), kind=kOutput, calls=%fused_computation.13 | convolution fusion | flops 510492672 | bytes 4423680 | tf_op jit(solution)/shard_map/dot_general | solution.py:43
  (15 shorter events, 0.7 us)
Async XLA Ops:
  0.0 3.0 %copy-start = (bf16[1,6,64,1152]{3,2,1,0:T(8,128)(2,1)S(1)}, bf16[1,6,64,1152]{3,2,1,0:T(8,128)(2,1)}, u32[]{:S(2)}) copy-start(bf16[1,6,64,1152]{3,2,1,0:T(8,128)(2,1)} %param.3) | copy-start | bytes 2654212
  59.4 1.9 copy-start.3
  180.2 3.4 %copy-start.1 = (bf16[48,8,8,72]{3,2,1,0:T(8,128)(2,1)S(1)}, bf16[48,8,8,72]{3,2,1,0:T(8,128)(2,1)}, u32[]{:S(2)}) copy-start(bf16[48,8,8,72]{3,2,1,0:T(8,128)(2,1)} %reshape.203) | copy-start | bytes 1327108
  183.6 3.7 %copy-start.2 = (bf16[48,8,8,72]{3,2,1,0:T(8,128)(2,1)S(1)}, bf16[48,8,8,72]{3,2,1,0:T(8,128)(2,1)}, u32[]{:S(2)}) copy-start(bf16[48,8,8,72]{3,2,1,0:T(8,128)(2,1)} %reshape.202) | copy-start | bytes 1327108
where the time goes:
time: 224 us; the launch traced here: 223 us
  blocking collectives  178 us (79%)
  matrix products  26.3 us (12%)
  local copies, waits for them, and re-layouts  14.9 us (7%)
  other arithmetic  3.82 us (2%)
    all_to_all x1, blocking collectives, per_device(): lax.all_to_all(joined, 'frame', split_axis=1, concat_axis=0, tiled=True)  87.1 us
    all_to_all x1, blocking collectives, per_device(): lax.all_to_all(joined, 'height', split_axis=2, concat_axis=1, tiled=True)  44.1 us
    all_to_all x1, blocking collectives, per_device(): lax.all_to_all(frames_att, 'frame', split_axis=0, concat_axis=1, tiled=True)  29.9 us
    all_to_all x1, blocking collectives, per_device(): lax.all_to_all(rows_att, 'height', split_axis=1, concat_axis=2, tiled=True)  17 us
    dot_general x2, matrix products, project(): joined = jnp.dot(flattened, weight, preferred_element_type=jnp.float32)  11.1 us
    sub x2, matrix products, attend(): scores = scores - jnp.max(scores, axis=-1, keepdims=True)  5.6 us
    dot_general x2, matrix products, residual(): jnp.dot(mixture.reshape(-1, mixture.shape[-1]), weight, preferred_element...  5.5 us

commit v1 on v0

v1 whole, which is shorter than its diff:
```python
import functools

import jax
import jax.numpy as jnp
from jax import lax
from jax.experimental import pallas as pl
from jax.experimental.pallas import tpu as pltpu
from jax.sharding import PartitionSpec as P

MESH = pl.DeviceIdType.MESH
BF16 = jnp.bfloat16
F32 = jnp.float32
HEAD_DIM = 72
SCALE = HEAD_DIM ** (-0.5)
GROUPS = (((0, 1, 2), 0), ((3,), 1), ((4, 5, 6), 2), ((7,), 3))


def layer_norm(values):
    center = values - jnp.mean(values, axis=-1, keepdims=True)
    spread = jnp.mean(center * center, axis=-1, keepdims=True)
    return (center * lax.rsqrt(spread + 1e-06)).astype(BF16)


def dot(a, b):
    return jnp.dot(a, b, preferred_element_type=F32)


def ones_where(condition):
    return jnp.where(condition, 1.0, 0.0).astype(BF16)


def iotas(rows, columns):
    shape = (rows, columns)
    return lax.broadcasted_iota(jnp.int32, shape, 0), lax.broadcasted_iota(jnp.int32, shape, 1)


def attend(q, k, v, same):
    tiles = [None] * 5
    for heads, first in GROUPS:
        window = slice(128 * first, 128 * first + 256)
        lane = lax.broadcasted_iota(jnp.int32, (1, 256), 1) + 128 * first
        masks = [
            jnp.where((lane >= HEAD_DIM * h) & (lane < HEAD_DIM * (h + 1)), 1.0, 0.0) for h in heads
        ]
        queries = q[:, window]
        stacked = jnp.concatenate([queries * m.astype(BF16) for m in masks], axis=0)
        scores = (
            lax.dot_general(
                stacked, k[:, window], (((1,), (1,)), ((), ())), preferred_element_type=F32
            )
            * SCALE
        )
        if same is not None:
            scores = jnp.where(same(*scores.shape), scores, -1e30)
        scores = scores - jnp.max(scores, axis=-1, keepdims=True)
        exponent = jnp.exp(scores)
        weights = (exponent / jnp.sum(exponent, axis=-1, keepdims=True)).astype(BF16)
        mixed = dot(weights, v[:, window])
        rows = q.shape[0]
        total = None
        for i, m in enumerate(masks):
            part = mixed[i * rows : (i + 1) * rows] * m
            total = part if total is None else total + part
        for half in range(2):
            part = total[:, 128 * half : 128 * half + 128]
            t = first + half
            tiles[t] = part if tiles[t] is None else tiles[t] + part
    return jnp.concatenate(tiles, axis=1)[:, :576].astype(BF16)


def same_row(rows, columns):
    a, b = iotas(rows, columns)
    return (a & 7) == (b & 7)


def kernel(
    lat, wqkv, wout, out,
    w0, w1, o0, o1,
    turn, back, sel, ext, unsel, unext,
    s1, r1, mid, s2, r2, qa, ka, va, qb, kb, vb, s3, r3, s4, r4,
    wsem, send1, recv1, send2, recv2, send3, recv3, send4, recv4,
):
    f, h = lax.axis_index("frame"), lax.axis_index("height")
    z, ylo = lax.rem(f, 12), lax.div(f, 12)
    yhi, xc = lax.div(h, 8), lax.rem(h, 8)
    x, c = lax.div(xc, 2), lax.rem(xc, 2)
    y = yhi * 4 + ylo
    column = y * 8 + xc

    loads = [
        pltpu.make_async_copy(wqkv.at[0], w0, wsem.at[0]),
        pltpu.make_async_copy(wout.at[0], o0, wsem.at[1]),
        pltpu.make_async_copy(wqkv.at[1], w1, wsem.at[2]),
        pltpu.make_async_copy(wout.at[1], o1, wsem.at[3]),
    ]
    for load in loads:
        load.start()

    def plane(dx, dy, dc):
        tx, ty, tc = lax.rem(x + dx, 4), lax.rem(y + dy, 8), lax.rem(c + dc, 2)
        th = lax.div(ty, 4) * 8 + tx * 2 + tc
        return (lax.rem(ty, 4) * 12 + z, th), th, ty * 8 + tx * 2 + tc

    def ring(dz):
        tz = lax.rem(z + dz, 12)
        return (ylo * 12 + tz, h), tz

    barrier = pltpu.get_barrier_semaphore()

    @pl.loop(1, 64)
    def _(o):
        device, _, _ = plane(lax.rem(lax.div(o, 2), 4), lax.div(o, 8), lax.rem(o, 2))
        pl.semaphore_signal(barrier, inc=1, device_id=device, device_id_type=MESH)

    @pl.loop(1, 12)
    def _(o):
        device, _ = ring(o)
        pl.semaphore_signal(barrier, inc=1, device_id=device, device_id_type=MESH)

    a, b = iotas(512, 512)
    turn[...] = ones_where(b == (a & 7) * 64 + (a >> 3))
    for t in range(0, 7, 2):
        wide = 256 if t < 6 else 128
        lanes = slice(128 * t, 128 * t + wide)
        rows = [lat[0, s, :, lanes] for s in range(6)]
        if t < 6:
            for first in (896, 1024):
                rows.append(
                    jnp.concatenate([lat[0, t + i, :, first : first + 128] for i in range(2)], axis=1)
                )
        else:
            rows.append(jnp.zeros((128, 128), BF16))
        packed = dot(turn[...], jnp.concatenate(rows, axis=0)).astype(BF16)
        s1[:, :, lanes] = packed.reshape(64, 8, wide)

    pl.semaphore_wait(barrier, 74)

    @pl.loop(0, 4)
    def _(k):
        @pl.loop(0, 16)
        def _(i):
            o = 15 - i
            device, _, there = plane(lax.rem(lax.div(o, 2), 4), k + 4 * lax.div(o, 8), lax.rem(o, 2))
            local = (k == 0) & (o == 0)

            @pl.when(jnp.logical_not(local))
            def _():
                pltpu.make_async_remote_copy(
                    src_ref=s1.at[there], dst_ref=r1.at[k, h],
                    send_sem=send1.at[k], recv_sem=recv1.at[k],
                    device_id=device, device_id_type=MESH,
                ).start()

            @pl.when(local)
            def _():
                pltpu.make_async_copy(s1.at[there], r1.at[k, h], recv1.at[k]).start()

    a, b = iotas(512, 512)
    back[...] = ones_where(b == (a & 63) * 8 + (a >> 6))
    a, b = iotas(96, 128)
    sel[...] = ones_where(((b & 7) < 6) & (a == (b >> 3) * 6 + (b & 7)))
    a, b = iotas(96, 768)
    place = a == ((b & 127) >> 3) * 6 + (b >> 7)
    ext[0:96, :] = ones_where(((b & 7) == 6) & place)
    ext[96:192, :] = ones_where(((b & 7) == 7) & place)
    a, b = iotas(128, 96)
    unsel[...] = ones_where(((a & 7) < 6) & (b == (a >> 3) * 6 + (a & 7)))
    a, b = iotas(768, 96)
    unext[...] = ones_where(((a & 7) >= 6) & (b == ((a & 127) >> 3) * 6 + (a >> 7)))
    va[...] = jnp.zeros_like(va)
    vb[...] = jnp.zeros_like(vb)

    def send_ring(k, source, target, send, recv):
        @pl.loop(0, 12)
        def _(i):
            o = lax.rem(i + 6, 12)
            device, tz = ring(o)

            @pl.when(o != 0)
            def _():
                pltpu.make_async_remote_copy(
                    src_ref=source.at[k, tz], dst_ref=target.at[k, z],
                    send_sem=send.at[k], recv_sem=recv.at[k],
                    device_id=device, device_id_type=MESH,
                ).start()

            @pl.when(o == 0)
            def _():
                pltpu.make_async_copy(source.at[k, tz], target.at[k, z], recv.at[k]).start()

    loads[0].wait()
    loads[1].wait()

    @pl.loop(0, 4)
    def _(k):
        pltpu.make_async_copy(r1.at[k], r1.at[k], recv1.at[k]).wait()
        got = r1[k].reshape(128, 896)
        tall = jnp.concatenate([got[:, 128 * t : 128 * t + 128] for t in range(6)], axis=0)
        end = dot(ext[...], tall)
        tokens = jnp.concatenate([dot(sel[...], got), end[0:96], end[96:192]], axis=1)
        joined = dot(layer_norm(tokens), w0[...]).astype(BF16)
        qa[...] = joined[:, 0:640]
        ka[...] = joined[:, 576:1216]
        va[:, 0:576] = joined[:, 1152:1728]
        mix = attend(qa[...], ka[...], va[...], None)
        middle = (tokens + dot(mix, o0[...])).astype(BF16)
        mid[k] = middle
        s2[k] = layer_norm(middle.astype(F32)).reshape(12, 8, 1152)
        send_ring(k, s2, r2, send2, recv2)

    loads[2].wait()

    @pl.loop(0, 4)
    def _(k):
        pltpu.make_async_copy(r2.at[k], r2.at[k], recv2.at[k]).wait()
        joined = dot(r2[k].reshape(96, 1152), w1[...]).astype(BF16)
        qb[k] = joined[:, 0:640]
        kb[k] = joined[:, 576:1216]
        vb[k, :, 0:576] = joined[:, 1152:1728]

    @pl.loop(0, 4)
    def _(k):
        mix = attend(qb[k], kb[...].reshape(384, 640), vb[...].reshape(384, 640), same_row)
        s3[k] = mix.reshape(12, 8, 576)
        send_ring(k, s3, r3, send3, recv3)

    loads[3].wait()

    @pl.loop(0, 4)
    def _(k):
        pltpu.make_async_copy(r3.at[k], r3.at[k], recv3.at[k]).wait()
        mix = r3[k].reshape(96, 576)
        result = (mid[k].astype(F32) + dot(mix, o1[...])).astype(BF16)
        main = dot(unsel[...], result[:, 0:896])
        end = dot(unext[...], result[:, 896:1152])
        sub = lax.broadcasted_iota(jnp.int32, (768, 128), 0) & 7
        end = jnp.where(sub == 6, end[:, 0:128], end[:, 128:256])
        tiles = [
            main[:, 128 * t : 128 * t + 128] + end[128 * t : 128 * t + 128] for t in range(6)
        ]
        tiles.append(main[:, 768:896])
        s4[k] = jnp.concatenate(tiles, axis=1).astype(BF16).reshape(16, 8, 896)

        @pl.loop(0, 16)
        def _(i):
            o = 15 - i
            device, th, _ = plane(
                lax.rem(lax.div(o, 2), 4), 8 - k + 4 * lax.div(o, 8), lax.rem(o, 2)
            )
            local = (k == 0) & (o == 0)

            @pl.when(jnp.logical_not(local))
            def _():
                pltpu.make_async_remote_copy(
                    src_ref=s4.at[k, th], dst_ref=r4.at[column],
                    send_sem=send4.at[k], recv_sem=recv4.at[0],
                    device_id=device, device_id_type=MESH,
                ).start()

            @pl.when(local)
            def _():
                pltpu.make_async_copy(s4.at[k, th], r4.at[column], recv4.at[0]).start()

    pltpu.make_async_copy(r4, r4, recv4.at[0]).wait()
    for t in range(0, 7, 2):
        wide = 256 if t < 6 else 128
        lanes = slice(128 * t, 128 * t + wide)
        turned = dot(back[...], r4[:, :, lanes].reshape(512, wide)).astype(BF16)
        for s in range(6):
            out[0, s, :, lanes] = turned[64 * s : 64 * s + 64]
        if t < 6:
            for i in range(2):
                part = turned[:, 128 * i : 128 * i + 128]
                out[0, t + i, :, 896:1024] = part[384:448]
                out[0, t + i, :, 1024:1152] = part[448:512]

    def sent(ref, sem):
        pltpu.make_async_copy(ref, ref, sem).wait()

    for k in range(4):
        plane_count = 15 if k == 0 else 16
        sent(r1.at[k, pl.ds(0, plane_count)], send1.at[k])
        sent(r2.at[k, pl.ds(0, 11)], send2.at[k])
        sent(r3.at[k, pl.ds(0, 11)], send3.at[k])
        sent(s4.at[k, pl.ds(0, plane_count)], send4.at[k])


def per_device(latents, qkv_weight, out_weight):
    vmem = pl.BlockSpec(memory_space=pltpu.VMEM)
    hbm = pl.BlockSpec(memory_space=pl.ANY)
    buffer = lambda *shape: pltpu.VMEM(shape, BF16)
    dma = pltpu.SemaphoreType.DMA
    return pl.pallas_call(
        kernel,
        out_shape=jax.ShapeDtypeStruct(latents.shape, BF16),
        in_specs=[vmem, hbm, hbm],
        out_specs=vmem,
        scratch_shapes=[
            buffer(1152, 1728), buffer(1152, 1728), buffer(576, 1152), buffer(576, 1152),
            buffer(512, 512), buffer(512, 512), buffer(96, 128), buffer(192, 768),
            buffer(128, 96), buffer(768, 96),
            buffer(64, 8, 896), buffer(4, 16, 8, 896), buffer(4, 96, 1152),
            buffer(4, 12, 8, 1152), buffer(4, 12, 8, 1152),
            buffer(96, 640), buffer(96, 640), buffer(96, 640),
            buffer(4, 96, 640), buffer(4, 96, 640), buffer(4, 96, 640),
            buffer(4, 12, 8, 576), buffer(4, 12, 8, 576),
            buffer(4, 16, 8, 896), buffer(64, 8, 896),
            dma((4,)), dma((4,)), dma((4,)), dma((4,)), dma((4,)), dma((4,)), dma((4,)),
            dma((4,)), dma((1,)),
        ],
        compiler_params=pltpu.CompilerParams(
            collective_id=0, has_side_effects=True, vmem_limit_bytes=56 * 2**20
        ),
        cost_estimate=pl.CostEstimate(
            flops=5_000_000_000, bytes_accessed=13_000_000, transcendentals=1_500_000
        ),
        name="axial_layer",
    )(latents, qkv_weight, out_weight)


def solution(mesh):
    return jax.shard_map(
        per_device,
        mesh=mesh,
        in_specs=(P("frame", "height", None, None), P(), P()),
        out_specs=P("frame", "height", None, None),
        check_vma=False,
    )
```

time: 224 us -> 116 us (0.52)
  blocking collectives: 178 us -> 0 us
  Pallas kernels: 0 us -> 102 us
  matrix products: 26.3 us -> 0 us
  other arithmetic: 3.82 us -> 0 us
    all_to_all x4 -> x0, blocking collectives: 178 us -> none  [the longest x1 87.1 us: per_device(): lax.all_to_all(joined, 'frame', split_axis=1, concat_axis=0, tiled=True)]
    pallas_call x0 -> x1, Pallas kernels: none -> 102 us  [per_device(): pl.pallas_call(kernel, out_shape=jax.ShapeDtypeStruct(latents.shape, BF16...]
    dot_general x6 -> x0, matrix products: 20.7 us -> none  [the longest x2 11.1 us: project(): joined = jnp.dot(flattened, weight, preferred_element_type=jnp.float32)]
    unnamed x8 -> x2, local copies, waits for them, and re-layouts: 0.01 us -> 13.7 us
    reshape x4 -> x0, local copies, waits for them, and re-layouts: 5.78 us -> none  [the longest x1 1.68 us: attend(): joined[:, :, 2 * inner_width:]]
    sub x2 -> x0, matrix products: 5.6 us -> none  [attend(): scores = scores - jnp.max(scores, axis=-1, keepdims=True)]
    convert_element_type x5 -> x0, local copies, waits for them, and re-layouts: 4.72 us -> none  [the longest x2 3.6 us: project(): joined.astype(jnp.bfloat16).reshape(tokens.shape[:-1] + (weight.shape[1],))]
    reduce_sum x3 -> x0, other arithmetic: 3.27 us -> none  [the longest x2 1.83 us: layer_norm(): spread = jnp.mean(center * center, axis=-1, keepdims=True)]
where the time goes in v1:
time: 116 us
  Pallas kernels  102 us (88%)
  local copies, waits for them, and re-layouts  13.7 us (12%)
    pallas_call x1, Pallas kernels, per_device(): pl.pallas_call(kernel, out_shape=jax.ShapeDtypeStruct(latents.shape, BF16...  102 us
    unnamed x2, local copies, waits for them, and re-layouts  13.7 us

profile of v1, /device:TPU:16, one launch (start us, length us, event | category | flops | bytes accessed | tf_op | source)
XLA Modules:
  0.0 115.6 jit_solution(13570903215711999517)
XLA Ops:
  0.0 11.6 %copy.4.wqkv = bf16[2,1152,1728]{2,1,0:T(8,128)(2,1)} copy(bf16[2,1152,1728]{1,2,0:T(8,128)(2,1)} %param.4) | data formatting | bytes 15925248 | tf_op args[1]
  11.6 101.9 %axial_layer.1 = bf16[1,6,64,1152]{3,2,1,0:T(8,128)(2,1)} custom-call(bf16[1,6,64,1152]{3,2,1,0:T(8,128)(2,1)} %lat.1, bf16[2,1152,1728]{2,1,0:T(8,128)(2,1)} %copy.4.wqkv, bf16[2,576,1152]{2,1,0:T(8,128)(2,1)} %wout.1), custom_call_target="tpu_custom_call" | custom-call | flops 5000000000 | bytes 13000000 | tf_op jit(solution)/shard_map/axial_layer/pallas_call | solution.py:293
  113.4 2.1 %copy.6 = bf16[1,6,64,1152]{3,2,1,0:T(8,128)(2,1)} copy(bf16[1,6,64,1152]{3,2,1,0:T(8,128)(2,1)} %axial_layer.1) | data formatting | bytes 1769472

commit v2 on v1

--- a/solution.py
+++ b/solution.py
@@ -23,6 +23,10 @@
 
 def dot(a, b):
     return jnp.dot(a, b, preferred_element_type=F32)
+
+
+def dot_t(a, b):
+    return lax.dot_general(a, b, (((1,), (1,)), ((), ())), preferred_element_type=F32)
 
 
 def ones_where(condition):
@@ -44,12 +48,7 @@
         ]
         queries = q[:, window]
         stacked = jnp.concatenate([queries * m.astype(BF16) for m in masks], axis=0)
-        scores = (
-            lax.dot_general(
-                stacked, k[:, window], (((1,), (1,)), ((), ())), preferred_element_type=F32
-            )
-            * SCALE
-        )
+        scores = dot_t(stacked, k[:, window]) * SCALE
         if same is not None:
             scores = jnp.where(same(*scores.shape), scores, -1e30)
         scores = scores - jnp.max(scores, axis=-1, keepdims=True)
@@ -65,7 +64,7 @@
             part = total[:, 128 * half : 128 * half + 128]
             t = first + half
             tiles[t] = part if tiles[t] is None else tiles[t] + part
-    return jnp.concatenate(tiles, axis=1)[:, :576].astype(BF16)
+    return jnp.concatenate(tiles, axis=1).astype(BF16)
 
 
 def same_row(rows, columns):
@@ -77,8 +76,8 @@
     lat, wqkv, wout, out,
     w0, w1, o0, o1,
     turn, back, sel, ext, unsel, unext,
-    s1, r1, mid, s2, r2, qa, ka, va, qb, kb, vb, s3, r3, s4, r4,
-    wsem, send1, recv1, send2, recv2, send3, recv3, send4, recv4,
+    s1, r1, mid, s2, r2, qa, ka, va, qb, kb, vb, s3, r3, s4, r4, s5, r5,
+    wsem, send1, recv1, send2, recv2, send3, recv3, send4, recv4, send5, recv5,
 ):
     f, h = lax.axis_index("frame"), lax.axis_index("height")
     z, ylo = lax.rem(f, 12), lax.div(f, 12)
@@ -139,7 +138,7 @@
     def _(k):
         @pl.loop(0, 16)
         def _(i):
-            o = 15 - i
+            o = 8 * lax.rem(i, 2) + 7 - lax.div(i, 2)
             device, _, there = plane(lax.rem(lax.div(o, 2), 4), k + 4 * lax.div(o, 8), lax.rem(o, 2))
             local = (k == 0) & (o == 0)
 
@@ -165,15 +164,21 @@
     ext[96:192, :] = ones_where(((b & 7) == 7) & place)
     a, b = iotas(128, 96)
     unsel[...] = ones_where(((a & 7) < 6) & (b == (a >> 3) * 6 + (a & 7)))
-    a, b = iotas(768, 96)
-    unext[...] = ones_where(((a & 7) >= 6) & (b == ((a & 127) >> 3) * 6 + (a >> 7)))
-    va[...] = jnp.zeros_like(va)
-    vb[...] = jnp.zeros_like(vb)
+    a, b = iotas(512, 96)
+    row, first, tile = a & 7, ((a & 127) >> 3) * 6, a >> 7
+    unext[...] = ones_where(
+        ((row == 6) & (b == first + tile)) | ((row == 7) & (tile < 2) & (b == first + 4 + tile))
+    )
+    for ref in (qa, ka, va):
+        ref[:, 512:640] = jnp.zeros((96, 128), BF16)
+    for ref in (qb, kb, vb):
+        ref[:, :, 512:640] = jnp.zeros((4, 96, 128), BF16)
 
     def send_ring(k, source, target, send, recv):
         @pl.loop(0, 12)
         def _(i):
-            o = lax.rem(i + 6, 12)
+            near = lax.div(i + 1, 2)
+            o = lax.rem(jnp.where(lax.rem(i, 2) == 1, 6 - near, 6 + near), 12)
             device, tz = ring(o)
 
             @pl.when(o != 0)
@@ -188,6 +193,50 @@
             def _():
                 pltpu.make_async_copy(source.at[k, tz], target.at[k, z], recv.at[k]).start()
 
+    def pack_mix(mix):
+        main = dot(unsel[...], mix[:, 0:512])
+        end = dot(unext[...], mix[:, 512:640])
+        tiles = [
+            main[:, 128 * t : 128 * t + 128] + end[128 * t : 128 * t + 128] for t in range(4)
+        ]
+        return jnp.concatenate(tiles, axis=1).astype(BF16).reshape(16, 8, 512)
+
+    def send_owners(k, source, target, send, recv):
+        @pl.loop(0, 16)
+        def _(i):
+            o = 8 * lax.rem(i, 2) + 7 - lax.div(i, 2)
+            device, th, _ = plane(
+                lax.rem(lax.div(o, 2), 4), 8 - k + 4 * lax.div(o, 8), lax.rem(o, 2)
+            )
+            local = (k == 0) & (o == 0)
+
+            @pl.when(jnp.logical_not(local))
+            def _():
+                pltpu.make_async_remote_copy(
+                    src_ref=source.at[k, th], dst_ref=target.at[column],
+                    send_sem=send.at[k], recv_sem=recv.at[0],
+                    device_id=device, device_id_type=MESH,
+                ).start()
+
+            @pl.when(local)
+            def _():
+                pltpu.make_async_copy(source.at[k, th], target.at[column], recv.at[0]).start()
+
+    def finish(arrived, recv, weight, base, target):
+        pltpu.make_async_copy(arrived, arrived, recv.at[0]).wait()
+        turned = dot(back[...], arrived[...].reshape(512, 512)).astype(BF16)
+        ends = [
+            turned[384 + 64 * (t // 4) :, 128 * (t % 4) : 128 * (t % 4) + 128][0:64]
+            for t in range(6)
+        ]
+        mix = jnp.concatenate([turned[0:384], jnp.concatenate(ends, axis=0)], axis=1)[:, 0:576]
+        for n in range(3):
+            lanes = slice(384 * n, 384 * n + 384)
+            update = dot(mix, weight[:, lanes])
+            for s in range(6):
+                rows = base[0, s, :, lanes].astype(F32) + update[64 * s : 64 * s + 64]
+                target[0, s, :, lanes] = rows.astype(BF16)
+
     loads[0].wait()
     loads[1].wait()
 
@@ -198,81 +247,41 @@
         tall = jnp.concatenate([got[:, 128 * t : 128 * t + 128] for t in range(6)], axis=0)
         end = dot(ext[...], tall)
         tokens = jnp.concatenate([dot(sel[...], got), end[0:96], end[96:192]], axis=1)
-        joined = dot(layer_norm(tokens), w0[...]).astype(BF16)
-        qa[...] = joined[:, 0:640]
-        ka[...] = joined[:, 576:1216]
-        va[:, 0:576] = joined[:, 1152:1728]
+        normed = layer_norm(tokens)
+        for part, ref in enumerate((qa, ka, va)):
+            ref[:, 0:576] = dot_t(normed, w0[576 * part : 576 * part + 576]).astype(BF16)
         mix = attend(qa[...], ka[...], va[...], None)
-        middle = (tokens + dot(mix, o0[...])).astype(BF16)
-        mid[k] = middle
+        middle = (tokens + dot(mix[:, 0:576], o0[...])).astype(BF16)
         s2[k] = layer_norm(middle.astype(F32)).reshape(12, 8, 1152)
         send_ring(k, s2, r2, send2, recv2)
+        s5[k] = pack_mix(mix)
+        send_owners(k, s5, r5, send5, recv5)
 
     loads[2].wait()
 
     @pl.loop(0, 4)
     def _(k):
         pltpu.make_async_copy(r2.at[k], r2.at[k], recv2.at[k]).wait()
-        joined = dot(r2[k].reshape(96, 1152), w1[...]).astype(BF16)
-        qb[k] = joined[:, 0:640]
-        kb[k] = joined[:, 576:1216]
-        vb[k, :, 0:576] = joined[:, 1152:1728]
+        normed = r2[k].reshape(96, 1152)
+        for part, ref in enumerate((qb, kb, vb)):
+            ref[k, :, 0:576] = dot_t(normed, w1[576 * part : 576 * part + 576]).astype(BF16)
 
     @pl.loop(0, 4)
     def _(k):
         mix = attend(qb[k], kb[...].reshape(384, 640), vb[...].reshape(384, 640), same_row)
-        s3[k] = mix.reshape(12, 8, 576)
+        s3[k] = mix.reshape(12, 8, 640)
         send_ring(k, s3, r3, send3, recv3)
 
+    finish(r5, recv5, o0, lat, mid)
     loads[3].wait()
 
     @pl.loop(0, 4)
     def _(k):
         pltpu.make_async_copy(r3.at[k], r3.at[k], recv3.at[k]).wait()
-        mix = r3[k].reshape(96, 576)
-        result = (mid[k].astype(F32) + dot(mix, o1[...])).astype(BF16)
-        main = dot(unsel[...], result[:, 0:896])
-        end = dot(unext[...], result[:, 896:1152])
-        sub = lax.broadcasted_iota(jnp.int32, (768, 128), 0) & 7
-        end = jnp.where(sub == 6, end[:, 0:128], end[:, 128:256])
-        tiles = [
-            main[:, 128 * t : 128 * t + 128] + end[128 * t : 128 * t + 128] for t in range(6)
-        ]
-        tiles.append(main[:, 768:896])
-        s4[k] = jnp.concatenate(tiles, axis=1).astype(BF16).reshape(16, 8, 896)
-
-        @pl.loop(0, 16)
-        def _(i):
-            o = 15 - i
-            device, th, _ = plane(
-                lax.rem(lax.div(o, 2), 4), 8 - k + 4 * lax.div(o, 8), lax.rem(o, 2)
-            )
-            local = (k == 0) & (o == 0)
-
-            @pl.when(jnp.logical_not(local))
-            def _():
-                pltpu.make_async_remote_copy(
-                    src_ref=s4.at[k, th], dst_ref=r4.at[column],
-                    send_sem=send4.at[k], recv_sem=recv4.at[0],
-                    device_id=device, device_id_type=MESH,
-                ).start()
-
-            @pl.when(local)
-            def _():
-                pltpu.make_async_copy(s4.at[k, th], r4.at[column], recv4.at[0]).start()
-
-    pltpu.make_async_copy(r4, r4, recv4.at[0]).wait()
-    for t in range(0, 7, 2):
-        wide = 256 if t < 6 else 128
-        lanes = slice(128 * t, 128 * t + wide)
-        turned = dot(back[...], r4[:, :, lanes].reshape(512, wide)).astype(BF16)
-        for s in range(6):
-            out[0, s, :, lanes] = turned[64 * s : 64 * s + 64]
-        if t < 6:
-            for i in range(2):
-                part = turned[:, 128 * i : 128 * i + 128]
-                out[0, t + i, :, 896:1024] = part[384:448]
-                out[0, t + i, :, 1024:1152] = part[448:512]
+        s4[k] = pack_mix(r3[k].reshape(96, 640))
+        send_owners(k, s4, r4, send4, recv4)
+
+    finish(r4, recv4, o1, mid, out)
 
     def sent(ref, sem):
         pltpu.make_async_copy(ref, ref, sem).wait()
@@ -283,6 +292,7 @@
         sent(r2.at[k, pl.ds(0, 11)], send2.at[k])
         sent(r3.at[k, pl.ds(0, 11)], send3.at[k])
         sent(s4.at[k, pl.ds(0, plane_count)], send4.at[k])
+        sent(s5.at[k, pl.ds(0, plane_count)], send5.at[k])
 
 
 def per_device(latents, qkv_weight, out_weight):
@@ -296,17 +306,17 @@
         in_specs=[vmem, hbm, hbm],
         out_specs=vmem,
         scratch_shapes=[
-            buffer(1152, 1728), buffer(1152, 1728), buffer(576, 1152), buffer(576, 1152),
+            buffer(1728, 1152), buffer(1728, 1152), buffer(576, 1152), buffer(576, 1152),
             buffer(512, 512), buffer(512, 512), buffer(96, 128), buffer(192, 768),
-            buffer(128, 96), buffer(768, 96),
-            buffer(64, 8, 896), buffer(4, 16, 8, 896), buffer(4, 96, 1152),
+            buffer(128, 96), buffer(512, 96),
+            buffer(64, 8, 896), buffer(4, 16, 8, 896), buffer(1, 6, 64, 1152),
             buffer(4, 12, 8, 1152), buffer(4, 12, 8, 1152),
             buffer(96, 640), buffer(96, 640), buffer(96, 640),
             buffer(4, 96, 640), buffer(4, 96, 640), buffer(4, 96, 640),
-            buffer(4, 12, 8, 576), buffer(4, 12, 8, 576),
-            buffer(4, 16, 8, 896), buffer(64, 8, 896),
+            buffer(4, 12, 8, 640), buffer(4, 12, 8, 640),
+            buffer(4, 16, 8, 512), buffer(64, 8, 512), buffer(4, 16, 8, 512), buffer(64, 8, 512),
             dma((4,)), dma((4,)), dma((4,)), dma((4,)), dma((4,)), dma((4,)), dma((4,)),
-            dma((4,)), dma((1,)),
+            dma((4,)), dma((1,)), dma((4,)), dma((1,)),
         ],
         compiler_params=pltpu.CompilerParams(
             collective_id=0, has_side_effects=True, vmem_limit_bytes=56 * 2**20
@@ -315,7 +325,7 @@
             flops=5_000_000_000, bytes_accessed=13_000_000, transcendentals=1_500_000
         ),
         name="axial_layer",
-    )(latents, qkv_weight, out_weight)
+    )(latents, jnp.swapaxes(qkv_weight, 1, 2), out_weight)
 
 
 def solution(mesh):

time: 116 us -> 98.2 us (0.85)
  the two profiles are of different devices: /device:TPU:16 before, /device:TPU:49 now
where the time goes in v2:
time: 98.2 us; the launch traced here: 98 us
  Pallas kernels  95.8 us (98%)
  local copies, waits for them, and re-layouts  2.15 us (2%)
    pallas_call x1, Pallas kernels, per_device(): pl.pallas_call(kernel, out_shape=jax.ShapeDtypeStruct(latents.shape, BF16...  95.8 us
    unnamed x1, local copies, waits for them, and re-layouts  2.15 us

profile of v2, /device:TPU:49, one launch (start us, length us, event | category | flops | bytes accessed | tf_op | source)
XLA Modules:
  0.0 98.0 jit_solution(9595079609837307243)
XLA Ops:
  0.0 95.8 %axial_layer.1 = bf16[1,6,64,1152]{3,2,1,0:T(8,128)(2,1)} custom-call(bf16[1,6,64,1152]{3,2,1,0:T(8,128)(2,1)} %lat.1, bf16[2,1728,1152]{2,1,0:T(8,128)(2,1)} %bitcast.1, bf16[2,576,1152]{2,1,0:T(8,128)(2,1)} %wout.1), custom_call_target="tpu_custom_call" | custom-call | flops 5000000000 | bytes 13000000 | tf_op jit(solution)/shard_map/axial_layer/pallas_call | solution.py:303
  95.8 2.1 %copy.5 = bf16[1,6,64,1152]{3,2,1,0:T(8,128)(2,1)} copy(bf16[1,6,64,1152]{3,2,1,0:T(8,128)(2,1)} %axial_layer.1) | data formatting | bytes 1769472

commit v3 on v2

--- a/solution.py
+++ b/solution.py
@@ -73,11 +73,11 @@
 
 
 def kernel(
-    lat, wqkv, wout, out,
-    w0, w1, o0, o1,
+    lat_hbm, wqkv, wout, out,
+    lat, result, w0, w1, o0, o1,
     turn, back, sel, ext, unsel, unext,
     s1, r1, mid, s2, r2, qa, ka, va, qb, kb, vb, s3, r3, s4, r4, s5, r5,
-    wsem, send1, recv1, send2, recv2, send3, recv3, send4, recv4, send5, recv5,
+    wsem, osem, send1, recv1, send2, recv2, send3, recv3, send4, recv4, send5, recv5,
 ):
     f, h = lax.axis_index("frame"), lax.axis_index("height")
     z, ylo = lax.rem(f, 12), lax.div(f, 12)
@@ -86,38 +86,61 @@
     y = yhi * 4 + ylo
     column = y * 8 + xc
 
+    entry = pltpu.make_async_copy(lat_hbm, lat, wsem.at[4])
+    entry.start()
     loads = [
         pltpu.make_async_copy(wqkv.at[0], w0, wsem.at[0]),
         pltpu.make_async_copy(wout.at[0], o0, wsem.at[1]),
         pltpu.make_async_copy(wqkv.at[1], w1, wsem.at[2]),
         pltpu.make_async_copy(wout.at[1], o1, wsem.at[3]),
     ]
+    across = [lax.rem(x + dx, 4) * 2 + lax.rem(c + dc, 2) for dx in range(4) for dc in range(2)]
+    around = [lax.rem(z + dz, 12) for dz in range(12)]
+
+    def level(dy):
+        ty = lax.rem(y + dy, 8)
+        return lax.rem(ty, 4) * 12 + z, lax.div(ty, 4) * 8, ty * 8
+
+    barrier = pltpu.get_barrier_semaphore()
+    for dy in range(8):
+        frame, height, _ = level(dy)
+        for i in range(8):
+            if dy or i:
+                pl.semaphore_signal(
+                    barrier, inc=1, device_id=(frame, height + across[i]), device_id_type=MESH
+                )
+    for dz in range(1, 12):
+        pl.semaphore_signal(
+            barrier, inc=1, device_id=(ylo * 12 + around[dz], h), device_id_type=MESH
+        )
     for load in loads:
         load.start()
 
-    def plane(dx, dy, dc):
-        tx, ty, tc = lax.rem(x + dx, 4), lax.rem(y + dy, 8), lax.rem(c + dc, 2)
-        th = lax.div(ty, 4) * 8 + tx * 2 + tc
-        return (lax.rem(ty, 4) * 12 + z, th), th, ty * 8 + tx * 2 + tc
-
-    def ring(dz):
-        tz = lax.rem(z + dz, 12)
-        return (ylo * 12 + tz, h), tz
-
-    barrier = pltpu.get_barrier_semaphore()
-
-    @pl.loop(1, 64)
-    def _(o):
-        device, _, _ = plane(lax.rem(lax.div(o, 2), 4), lax.div(o, 8), lax.rem(o, 2))
-        pl.semaphore_signal(barrier, inc=1, device_id=device, device_id_type=MESH)
-
-    @pl.loop(1, 12)
-    def _(o):
-        device, _ = ring(o)
-        pl.semaphore_signal(barrier, inc=1, device_id=device, device_id_type=MESH)
+    def send_plane(k, dy, source, target, send, recv):
+        levels = [level(dy), level(dy + 4)]
+        for i in range(16):
+            frame, height, first = levels[i % 2]
+            peer = 7 - i // 2
+            block = source(height + across[peer], first + across[peer])
+
+            def remote():
+                pltpu.make_async_remote_copy(
+                    src_ref=block, dst_ref=target, send_sem=send, recv_sem=recv,
+                    device_id=(frame, height + across[peer]), device_id_type=MESH,
+                ).start()
+
+            if peer or i % 2:
+                remote()
+            else:
+                pl.when(k != 0)(remote)
+
+                @pl.when(k == 0)
+                def _():
+                    pltpu.make_async_copy(block, target, recv).start()
 
     a, b = iotas(512, 512)
     turn[...] = ones_where(b == (a & 7) * 64 + (a >> 3))
+    entry.wait()
     for t in range(0, 7, 2):
         wide = 256 if t < 6 else 128
         lanes = slice(128 * t, 128 * t + wide)
@@ -136,23 +159,7 @@
 
     @pl.loop(0, 4)
     def _(k):
-        @pl.loop(0, 16)
-        def _(i):
-            o = 8 * lax.rem(i, 2) + 7 - lax.div(i, 2)
-            device, _, there = plane(lax.rem(lax.div(o, 2), 4), k + 4 * lax.div(o, 8), lax.rem(o, 2))
-            local = (k == 0) & (o == 0)
-
-            @pl.when(jnp.logical_not(local))
-            def _():
-                pltpu.make_async_remote_copy(
-                    src_ref=s1.at[there], dst_ref=r1.at[k, h],
-                    send_sem=send1.at[k], recv_sem=recv1.at[k],
-                    device_id=device, device_id_type=MESH,
-                ).start()
-
-            @pl.when(local)
-            def _():
-                pltpu.make_async_copy(s1.at[there], r1.at[k, h], recv1.at[k]).start()
+        send_plane(k, k, lambda _, there: s1.at[there], r1.at[k, h], send1.at[k], recv1.at[k])
 
     a, b = iotas(512, 512)
     back[...] = ones_where(b == (a & 63) * 8 + (a >> 6))
@@ -169,29 +176,17 @@
     unext[...] = ones_where(
         ((row == 6) & (b == first + tile)) | ((row == 7) & (tile < 2) & (b == first + 4 + tile))
     )
-    for ref in (qa, ka, va):
-        ref[:, 512:640] = jnp.zeros((96, 128), BF16)
-    for ref in (qb, kb, vb):
-        ref[:, :, 512:640] = jnp.zeros((4, 96, 128), BF16)
+    va[:, 512:640] = jnp.zeros((96, 128), BF16)
+    vb[:, :, 512:640] = jnp.zeros((4, 96, 128), BF16)
 
     def send_ring(k, source, target, send, recv):
-        @pl.loop(0, 12)
-        def _(i):
-            near = lax.div(i + 1, 2)
-            o = lax.rem(jnp.where(lax.rem(i, 2) == 1, 6 - near, 6 + near), 12)
-            device, tz = ring(o)
-
-            @pl.when(o != 0)
-            def _():
-                pltpu.make_async_remote_copy(
-                    src_ref=source.at[k, tz], dst_ref=target.at[k, z],
-                    send_sem=send.at[k], recv_sem=recv.at[k],
-                    device_id=device, device_id_type=MESH,
-                ).start()
-
-            @pl.when(o == 0)
-            def _():
-                pltpu.make_async_copy(source.at[k, tz], target.at[k, z], recv.at[k]).start()
+        for dz in (6, 5, 7, 4, 8, 3, 9, 2, 10, 1, 11):
+            pltpu.make_async_remote_copy(
+                src_ref=source.at[k, around[dz]], dst_ref=target.at[k, z],
+                send_sem=send.at[k], recv_sem=recv.at[k],
+                device_id=(ylo * 12 + around[dz], h), device_id_type=MESH,
+            ).start()
+        pltpu.make_async_copy(source.at[k, z], target.at[k, z], recv.at[k]).start()
 
     def pack_mix(mix):
         main = dot(unsel[...], mix[:, 0:512])
@@ -202,27 +197,18 @@
         return jnp.concatenate(tiles, axis=1).astype(BF16).reshape(16, 8, 512)
 
     def send_owners(k, source, target, send, recv):
-        @pl.loop(0, 16)
-        def _(i):
-            o = 8 * lax.rem(i, 2) + 7 - lax.div(i, 2)
-            device, th, _ = plane(
-                lax.rem(lax.div(o, 2), 4), 8 - k + 4 * lax.div(o, 8), lax.rem(o, 2)
-            )
-            local = (k == 0) & (o == 0)
-
-            @pl.when(jnp.logical_not(local))
-            def _():
-                pltpu.make_async_remote_copy(
-                    src_ref=source.at[k, th], dst_ref=target.at[column],
-                    send_sem=send.at[k], recv_sem=recv.at[0],
-                    device_id=device, device_id_type=MESH,
-                ).start()
-
-            @pl.when(local)
-            def _():
-                pltpu.make_async_copy(source.at[k, th], target.at[column], recv.at[0]).start()
-
-    def finish(arrived, recv, weight, base, target):
+        send_plane(
+            k, 8 - k, lambda there, _: source.at[k, there], target.at[column], send.at[k], recv.at[0]
+        )
+
+    exits = [
+        pltpu.make_async_copy(
+            result.at[:, :, :, pl.ds(384 * n, 384)], out.at[:, :, :, pl.ds(384 * n, 384)], osem.at[n]
+        )
+        for n in range(3)
+    ]
+
+    def finish(arrived, recv, weight, base, target, leave):
         pltpu.make_async_copy(arrived, arrived, recv.at[0]).wait()
         turned = dot(back[...], arrived[...].reshape(512, 512)).astype(BF16)
         ends = [
@@ -236,6 +222,8 @@
             for s in range(6):
                 rows = base[0, s, :, lanes].astype(F32) + update[64 * s : 64 * s + 64]
                 target[0, s, :, lanes] = rows.astype(BF16)
+            if leave:
+                exits[n].start()
 
     loads[0].wait()
     loads[1].wait()
@@ -247,9 +235,10 @@
         tall = jnp.concatenate([got[:, 128 * t : 128 * t + 128] for t in range(6)], axis=0)
         end = dot(ext[...], tall)
         tokens = jnp.concatenate([dot(sel[...], got), end[0:96], end[96:192]], axis=1)
-        normed = layer_norm(tokens)
-        for part, ref in enumerate((qa, ka, va)):
-            ref[:, 0:576] = dot_t(normed, w0[576 * part : 576 * part + 576]).astype(BF16)
+        joined = dot_t(layer_norm(tokens), w0[...]).astype(BF16)
+        qa[...] = joined[:, 0:640]
+        ka[...] = joined[:, 576:1216]
+        va[:, 0:576] = joined[:, 1152:1728]
         mix = attend(qa[...], ka[...], va[...], None)
         middle = (tokens + dot(mix[:, 0:576], o0[...])).astype(BF16)
         s2[k] = layer_norm(middle.astype(F32)).reshape(12, 8, 1152)
@@ -262,9 +251,10 @@
     @pl.loop(0, 4)
     def _(k):
         pltpu.make_async_copy(r2.at[k], r2.at[k], recv2.at[k]).wait()
-        normed = r2[k].reshape(96, 1152)
-        for part, ref in enumerate((qb, kb, vb)):
-            ref[k, :, 0:576] = dot_t(normed, w1[576 * part : 576 * part + 576]).astype(BF16)
+        joined = dot_t(r2[k].reshape(96, 1152), w1[...]).astype(BF16)
+        qb[k] = joined[:, 0:640]
+        kb[k] = joined[:, 576:1216]
+        vb[k, :, 0:576] = joined[:, 1152:1728]
 
     @pl.loop(0, 4)
     def _(k):
@@ -272,7 +262,7 @@
         s3[k] = mix.reshape(12, 8, 640)
         send_ring(k, s3, r3, send3, recv3)
 
-    finish(r5, recv5, o0, lat, mid)
+    finish(r5, recv5, o0, lat, mid, False)
     loads[3].wait()
 
     @pl.loop(0, 4)
@@ -281,7 +271,7 @@
         s4[k] = pack_mix(r3[k].reshape(96, 640))
         send_owners(k, s4, r4, send4, recv4)
 
-    finish(r4, recv4, o1, mid, out)
+    finish(r4, recv4, o1, mid, result, True)
 
     def sent(ref, sem):
         pltpu.make_async_copy(ref, ref, sem).wait()
@@ -293,19 +283,21 @@
         sent(r3.at[k, pl.ds(0, 11)], send3.at[k])
         sent(s4.at[k, pl.ds(0, plane_count)], send4.at[k])
         sent(s5.at[k, pl.ds(0, plane_count)], send5.at[k])
+    for leaving in exits:
+        leaving.wait()
 
 
 def per_device(latents, qkv_weight, out_weight):
-    vmem = pl.BlockSpec(memory_space=pltpu.VMEM)
     hbm = pl.BlockSpec(memory_space=pl.ANY)
     buffer = lambda *shape: pltpu.VMEM(shape, BF16)
     dma = pltpu.SemaphoreType.DMA
     return pl.pallas_call(
         kernel,
         out_shape=jax.ShapeDtypeStruct(latents.shape, BF16),
-        in_specs=[vmem, hbm, hbm],
-        out_specs=vmem,
+        in_specs=[hbm, hbm, hbm],
+        out_specs=hbm,
         scratch_shapes=[
+            buffer(1, 6, 64, 1152), buffer(1, 6, 64, 1152),
             buffer(1728, 1152), buffer(1728, 1152), buffer(576, 1152), buffer(576, 1152),
             buffer(512, 512), buffer(512, 512), buffer(96, 128), buffer(192, 768),
             buffer(128, 96), buffer(512, 96),
@@ -315,7 +307,8 @@
             buffer(4, 96, 640), buffer(4, 96, 640), buffer(4, 96, 640),
             buffer(4, 12, 8, 640), buffer(4, 12, 8, 640),
             buffer(4, 16, 8, 512), buffer(64, 8, 512), buffer(4, 16, 8, 512), buffer(64, 8, 512),
-            dma((4,)), dma((4,)), dma((4,)), dma((4,)), dma((4,)), dma((4,)), dma((4,)),
+            dma((5,)), dma((3,)),
+            dma((4,)), dma((4,)), dma((4,)), dma((4,)), dma((4,)), dma((4,)),
             dma((4,)), dma((1,)), dma((4,)), dma((1,)),
         ],
         compiler_params=pltpu.CompilerParams(

time: 98.2 us -> 95.4 us (0.971)
  the two profiles are of different devices: /device:TPU:49 before, /device:TPU:16 now
where the time goes in v3:
time: 95.4 us; the launch traced here: 95.3 us
  Pallas kernels  93.1 us (98%)
  local copies, waits for them, and re-layouts  2.15 us (2%)
    pallas_call x1, Pallas kernels, per_device(): pl.pallas_call(kernel, out_shape=jax.ShapeDtypeStruct(latents.shape, BF16...  93.1 us
    unnamed x1, local copies, waits for them, and re-layouts  2.15 us

profile of v3, /device:TPU:16, one launch (start us, length us, event | category | flops | bytes accessed | tf_op | source)
XLA Modules:
  0.0 95.3 jit_solution(10021399668399153915)
XLA Ops:
  0.0 93.1 %axial_layer.1 = bf16[1,6,64,1152]{3,2,1,0:T(8,128)(2,1)} custom-call(bf16[1,6,64,1152]{3,2,1,0:T(8,128)(2,1)} %lat_hbm.1, bf16[2,1728,1152]{2,1,0:T(8,128)(2,1)} %bitcast.1, bf16[2,576,1152]{2,1,0:T(8,128)(2,1)} %wout.1), custom_call_target="tpu_custom_call" | custom-call | flops 5000000000 | bytes 13000000 | tf_op jit(solution)/shard_map/axial_layer/pallas_call | solution.py:294
  93.1 2.1 %copy.5 = bf16[1,6,64,1152]{3,2,1,0:T(8,128)(2,1)} copy(bf16[1,6,64,1152]{3,2,1,0:T(8,128)(2,1)} %axial_layer.1) | data formatting | bytes 1769472

commit v4 on v3

--- a/solution.py
+++ b/solution.py
@@ -53,7 +53,7 @@
             scores = jnp.where(same(*scores.shape), scores, -1e30)
         scores = scores - jnp.max(scores, axis=-1, keepdims=True)
         exponent = jnp.exp(scores)
-        weights = (exponent / jnp.sum(exponent, axis=-1, keepdims=True)).astype(BF16)
+        weights = (exponent * (1.0 / jnp.sum(exponent, axis=-1, keepdims=True))).astype(BF16)
         mixed = dot(weights, v[:, window])
         rows = q.shape[0]
         total = None
@@ -119,8 +119,9 @@
     def send_plane(k, dy, source, target, send, recv):
         levels = [level(dy), level(dy + 4)]
         for i in range(16):
-            frame, height, first = levels[i % 2]
-            peer = 7 - i // 2
+            farther = 1 - i % 2
+            frame, height, first = levels[farther]
+            peer = (4, 5, 2, 6, 3, 7, 1, 0)[i // 2]
             block = source(height + across[peer], first + across[peer])
 
             def remote():
@@ -129,7 +130,7 @@
                     device_id=(frame, height + across[peer]), device_id_type=MESH,
                 ).start()
 
-            if peer or i % 2:
+            if peer or farther:
                 remote()
             else:
                 pl.when(k != 0)(remote)

time: 95.4 us -> 95.9 us (level)
  no operation moved by 1% of the time
where the time goes in v4:
time: 95.9 us; the launch traced here: 95.5 us
  Pallas kernels  93.3 us (97%)
  local copies, waits for them, and re-layouts  2.15 us (2%)
    pallas_call x1, Pallas kernels, per_device(): pl.pallas_call(kernel, out_shape=jax.ShapeDtypeStruct(latents.shape, BF16...  93.3 us
    unnamed x1, local copies, waits for them, and re-layouts  2.15 us

profile of v4, /device:TPU:16, one launch (start us, length us, event | category | flops | bytes accessed | tf_op | source)
XLA Modules:
  0.0 95.5 jit_solution(117503137349672179)
XLA Ops:
  0.0 93.3 %axial_layer.1 = bf16[1,6,64,1152]{3,2,1,0:T(8,128)(2,1)} custom-call(bf16[1,6,64,1152]{3,2,1,0:T(8,128)(2,1)} %lat_hbm.1, bf16[2,1728,1152]{2,1,0:T(8,128)(2,1)} %bitcast.1, bf16[2,576,1152]{2,1,0:T(8,128)(2,1)} %wout.1), custom_call_target="tpu_custom_call" | custom-call | flops 5000000000 | bytes 13000000 | tf_op jit(solution)/shard_map/axial_layer/pallas_call | solution.py:295
  93.3 2.1 %copy.5 = bf16[1,6,64,1152]{3,2,1,0:T(8,128)(2,1)} copy(bf16[1,6,64,1152]{3,2,1,0:T(8,128)(2,1)} %axial_layer.1) | data formatting | bytes 1769472
